TPU v7x, 32 devices: a whole 2x2x4 slice. The times are simulated.
32 devices in a mesh: replica: 4 (over x, core), expert: 8 (over z, y).
Axes of the slice: x: 2, y: 2, z: 4, core: 2. Of those that a mesh axis runs over, the one named last changes fastest.
Arguments:
- tokens: bfloat16 [4, 1024, 4096], P('replica', 'expert'), may hold values from -4 to 4
- routes: int32 [4, 1024, 8], P('replica', 'expert'), may hold values from 0 to 127, as said below
- cweights: float32 [4, 1024, 8], P('replica', 'expert'), may hold values from 0.1 to 1
- w_gate: bfloat16 [4, 4096, 1024], P('replica', None, 'expert'), may hold values from -0.09375 to 0.09375
- w_up: bfloat16 [4, 4096, 1024], P('replica', None, 'expert'), may hold values from -0.09375 to 0.09375
- w_down: bfloat16 [4, 1024, 4096], P('replica', 'expert'), may hold values from -0.1875 to 0.1875
- grad_out: bfloat16 [4, 1024, 4096], P('replica', 'expert'), may hold values from -4 to 4
- frag_local: bfloat16 [4, 2, 1024, 4096], P('replica', None, 'expert'), may hold values from -2000 to 2000
- frag_global: float32 [2, 1024, 4096], P(None, 'expert', 'replica'), may hold values from -2 to 2
- frag_moment: float32 [2, 1024, 4096], P(None, 'expert', 'replica'), may hold values from -4 to 4
Outputs:
- layer_out: bfloat16 [4, 1024, 4096], P('replica', 'expert')
- grad_tokens: bfloat16 [4, 1024, 4096], P('replica', 'expert')
- grad_gate: bfloat16 [4, 4096, 1024], P('replica', None, 'expert')
- grad_up: bfloat16 [4, 4096, 1024], P('replica', None, 'expert')
- grad_down: bfloat16 [4, 1024, 4096], P('replica', 'expert')
- new_global: float32 [2, 1024, 4096], P(None, 'expert', 'replica')
- new_moment: float32 [2, 1024, 4096], P(None, 'expert', 'replica')
- new_local: bfloat16 [4, 2, 1024, 4096], P('replica', None, 'expert')
Inputs may be any that keep to these rules, and one draw needn't show every extreme that they name: `routes`: ids in a row are distinct. In each block of 128 rows of one device, each id below 1 is named by at most 32 rows; in every draw one id below 1 is named by exactly 32 rows in every block.
All inputs are finite; a program needn't handle non-finite values.
Results may differ from a plain program's by a relative error of at most 0.009.
Values may be sent and summed in bfloat16 or wider, within the bound.
A program may use at most 128 MiB of HBM per device.

v0:
```python
import jax
import jax.numpy as jnp
from jax import lax
from jax.sharding import PartitionSpec as P

D = 4096
HID = 1024
SPLIT = 8
CAP = 32


OUTER_MOMENTUM = 0.9
OUTER_RATE = 0.7
CLIP_RMS = 0.5


def silu_parts(gate_pre):
    sigmoid_val = jax.nn.sigmoid(gate_pre)
    return (gate_pre * sigmoid_val, sigmoid_val * (1.0 + gate_pre * (1.0 - sigmoid_val)))


def outer_update(pseudo, squares, moment, anchor):
    clip_limit = CLIP_RMS * (HID * D) ** 0.5
    factor = jnp.minimum(jnp.float32(1.0), clip_limit / (jnp.sqrt(squares) + 1e-06))
    clipped = pseudo * factor[:, None, None]
    moment_next = OUTER_MOMENTUM * moment + clipped
    anchor_next = anchor - OUTER_RATE * (OUTER_MOMENTUM * moment_next + clipped)
    return (moment_next, anchor_next)


def body(
    tokens, routes, cweights, w_gate, w_up, w_down, grad_out, frag_local, frag_global, frag_moment
):
    groups = lax.axis_size("expert")
    window = groups // SPLIT
    precise = lax.Precision.HIGHEST
    inputs = tokens[0]
    grads_in = grad_out[0]
    route_ids = routes[0]
    weights = cweights[0]
    wg_part = w_gate[0]
    wu_part = w_up[0]
    wd_part = w_down[0]
    model_width = inputs.shape[1]
    experts = jnp.arange(window, dtype=jnp.int32)
    matched = route_ids[:, :, None] == experts[None, None, :]
    routed = jnp.any(matched, axis=1).astype(jnp.int32)
    shares = jnp.sum(jnp.where(matched, weights[:, :, None], jnp.float32(0.0)), axis=1)
    places = jnp.cumsum(routed, axis=0) - 1
    slot_ids = jnp.arange(CAP, dtype=jnp.int32)
    layout = (routed.T[:, None, :] == 1) & (places.T[:, None, :] == slot_ids[None, :, None])
    layout_f = layout.astype(jnp.float32)
    layout_b = layout.astype(jnp.bfloat16)
    combine = layout_f * shares.T[:, None, :]
    slot_share = jnp.sum(combine, axis=2)
    picked = jnp.einsum("ect,td->ecd", layout_b, inputs, preferred_element_type=jnp.float32).astype(
        jnp.bfloat16
    )
    outbound = jnp.broadcast_to(picked[:, None], (window, SPLIT, CAP, model_width)).reshape(
        groups, CAP, model_width
    )
    received = lax.all_to_all(outbound, "expert", split_axis=0, concat_axis=0, tiled=True)
    n_source, n_rows, width_in = received.shape
    flat = received.reshape(n_source * n_rows, width_in)
    gate_pre = jnp.dot(flat, wg_part, preferred_element_type=jnp.float32)
    up_pre = jnp.dot(flat, wu_part, preferred_element_type=jnp.float32)
    silu_val, silu_slope = silu_parts(gate_pre)
    hidden_act = (silu_val * up_pre).astype(jnp.bfloat16)
    partial_value = jnp.dot(hidden_act, wd_part, preferred_element_type=jnp.float32)
    partial_out, hidden_act, gate_pre, up_pre, rows_in = (
        partial_value.reshape(n_source, n_rows, width_in),
        hidden_act.reshape(n_source, n_rows, -1),
        gate_pre.reshape(n_source, n_rows, -1),
        up_pre.reshape(n_source, n_rows, -1),
        received,
    )
    returned = lax.all_to_all(partial_out, "expert", split_axis=0, concat_axis=0, tiled=True)
    expert_out = jnp.sum(returned.reshape(window, SPLIT, CAP, model_width), axis=1)
    layer_out = jnp.einsum(
        "ect,ecd->td", combine, expert_out, precision=precise, preferred_element_type=jnp.float32
    ).astype(jnp.bfloat16)
    dy_picked = jnp.einsum("ect,td->ecd", layout_b, grads_in, preferred_element_type=jnp.float32)
    dy_scaled = (dy_picked * slot_share[:, :, None]).astype(jnp.bfloat16)
    outbound_dy = jnp.broadcast_to(dy_scaled[:, None], (window, SPLIT, CAP, model_width)).reshape(
        groups, CAP, model_width
    )
    rows_dy = lax.all_to_all(outbound_dy, "expert", split_axis=0, concat_axis=0, tiled=True)
    grad_rows = rows_dy.reshape(-1, model_width)
    tok_rows = rows_in.reshape(-1, model_width)
    act_rows = hidden_act.reshape(grad_rows.shape[0], -1)
    gate_rows = gate_pre.reshape(grad_rows.shape[0], -1)
    up_rows = up_pre.reshape(grad_rows.shape[0], -1)
    grad_hidden = jnp.einsum("rd,hd->rh", grad_rows, wd_part, preferred_element_type=jnp.float32)
    silu_val, silu_slope = silu_parts(gate_rows)
    grad_gate_pre = (grad_hidden * up_rows * silu_slope).astype(jnp.bfloat16)
    grad_up_pre = (grad_hidden * silu_val).astype(jnp.bfloat16)
    grad_gate = jnp.einsum(
        "rd,rh->dh", tok_rows, grad_gate_pre, preferred_element_type=jnp.float32
    ).astype(jnp.bfloat16)[None]
    grad_up = jnp.einsum(
        "rd,rh->dh", tok_rows, grad_up_pre, preferred_element_type=jnp.float32
    ).astype(jnp.bfloat16)[None]
    grad_down = jnp.einsum(
        "rh,rd->hd", act_rows, grad_rows, preferred_element_type=jnp.float32
    ).astype(jnp.bfloat16)[None]
    partial_dx = jnp.einsum(
        "rh,dh->rd", grad_gate_pre, wg_part, preferred_element_type=jnp.float32
    ) + jnp.einsum("rh,dh->rd", grad_up_pre, wu_part, preferred_element_type=jnp.float32)
    partial_dx = partial_dx.reshape(groups, CAP, model_width)
    returned_dx = lax.all_to_all(partial_dx, "expert", split_axis=0, concat_axis=0, tiled=True)
    expert_dx = jnp.sum(returned_dx.reshape(window, SPLIT, CAP, model_width), axis=1)
    grad_tokens = jnp.einsum(
        "ect,ecd->td", layout_f, expert_dx, precision=precise, preferred_element_type=jnp.float32
    ).astype(jnp.bfloat16)
    replicas = lax.axis_size("replica")
    local_terms = frag_local[0].astype(jnp.float32)
    summed = lax.psum_scatter(
        local_terms.astype(jnp.bfloat16), "replica", scatter_dimension=2, tiled=True
    ).astype(jnp.float32)
    pseudo = frag_global - summed / replicas
    squares = lax.psum(jnp.sum(pseudo * pseudo, axis=(1, 2)), ("replica", "expert"))
    new_moment, new_global = outer_update(pseudo, squares, frag_moment, frag_global)
    new_local = lax.all_gather(new_global.astype(jnp.bfloat16), "replica", axis=2, tiled=True)[None]
    return (
        layer_out[None],
        grad_tokens[None],
        grad_gate,
        grad_up,
        grad_down,
        new_global,
        new_moment,
        new_local,
    )


def solution(mesh):
    return jax.shard_map(
        body,
        mesh=mesh,
        in_specs=(
            P("replica", "expert", None),
            P("replica", "expert", None),
            P("replica", "expert", None),
            P("replica", None, "expert"),
            P("replica", None, "expert"),
            P("replica", "expert", None),
            P("replica", "expert", None),
            P("replica", None, "expert", None),
            P(None, "expert", "replica"),
            P(None, "expert", "replica"),
        ),
        out_specs=(
            P("replica", "expert", None),
            P("replica", "expert", None),
            P("replica", None, "expert"),
            P("replica", None, "expert"),
            P("replica", "expert", None),
            P(None, "expert", "replica"),
            P(None, "expert", "replica"),
            P("replica", None, "expert", None),
        ),
        check_vma=False,
    )
```

profile of v0, /device:TPU:16, one launch (start us, length us, event | category | flops | bytes accessed | tf_op | source)
XLA Modules:
  0.0 384.6 jit_solution(8088277371795552086)
XLA Ops:
  9.9 1.6 reshape.289
  11.5 6.2 %all-to-all-start = ((bf16[8,32,4096]{2,1,0:T(8,128)(2,1)}), bf16[8,32,4096]{2,1,0:T(8,128)(2,1)S(1)}, u32[]{:S(2)}, u32[]{:S(2)}) async-start(bf16[8,32,4096]{2,1,0:T(8,128)(2,1)} %reshape.289), calls=%async_computation | async-start | bytes 4194304 | tf_op jit(solution)/shard_map/all_to_all | solution.py:62
  19.3 43.3 %all-to-all-done = bf16[8,32,4096]{2,1,0:T(8,128)(2,1)S(1)} async-done(((bf16[8,32,4096]{2,1,0:T(8,128)(2,1)}), bf16[8,32,4096]{2,1,0:T(8,128)(2,1)S(1)}, u32[]{:S(2)}, u32[]{:S(2)}) %all-to-all-start) | async-done | bytes 2097184 | tf_op jit(solution)/shard_map/all_to_all | solution.py:62
  64.2 7.5 %all-to-all-start.2 = ((bf16[8,32,4096]{2,1,0:T(8,128)(2,1)}), bf16[8,32,4096]{2,1,0:T(8,128)(2,1)}, u32[]{:S(2)}, u32[]{:S(2)}) async-start(bf16[8,32,4096]{2,1,0:T(8,128)(2,1)} %reshape.291), calls=%async_computation.2 | async-start | bytes 4194304 | tf_op jit(solution)/shard_map/all_to_all | solution.py:87
  71.7 2.0 fusion.16
  75.1 41.2 %all-to-all-done.2 = bf16[8,32,4096]{2,1,0:T(8,128)(2,1)} async-done(((bf16[8,32,4096]{2,1,0:T(8,128)(2,1)}), bf16[8,32,4096]{2,1,0:T(8,128)(2,1)}, u32[]{:S(2)}, u32[]{:S(2)}) %all-to-all-start.2) | async-done | bytes 2097184 | tf_op jit(solution)/shard_map/all_to_all | solution.py:87
  116.2 2.3 multiply_convert_fusion
  118.5 2.7 fusion.7
  121.2 7.8 %all-to-all-start.1 = ((f32[8,32,4096]{2,1,0:T(8,128)}), f32[8,32,4096]{2,1,0:T(8,128)}, u32[]{:S(2)}, u32[]{:S(2)}) async-start(f32[8,32,4096]{2,1,0:T(8,128)} %fusion.7), calls=%async_computation.1 | async-start | bytes 8388608 | tf_op jit(solution)/shard_map/all_to_all | solution.py:77
  129.8 2.0 fusion.14
  131.8 2.7 convolution_add_fusion
  134.5 83.8 %all-to-all-done.1 = f32[8,32,4096]{2,1,0:T(8,128)} async-done(((f32[8,32,4096]{2,1,0:T(8,128)}), f32[8,32,4096]{2,1,0:T(8,128)}, u32[]{:S(2)}, u32[]{:S(2)}) %all-to-all-start.1) | async-done | bytes 4194336 | tf_op jit(solution)/shard_map/all_to_all | solution.py:77
  218.3 7.9 %all-to-all-start.3 = ((f32[8,32,4096]{2,1,0:T(8,128)}), f32[8,32,4096]{2,1,0:T(8,128)}, u32[]{:S(2)}, u32[]{:S(2)}) async-start(f32[8,32,4096]{2,1,0:T(8,128)} %bitcast.60), calls=%async_computation.3 | async-start | bytes 8388608 | tf_op jit(solution)/shard_map/all_to_all | solution.py:110
  226.2 1.7 multiply_reduce_fusion
  227.9 109.0 %psum.7 = f32[2]{0:T(128)S(1)} all-reduce(f32[2]{0:T(128)S(1)} %multiply_reduce_fusion), channel_id=1, replica_groups=mesh['replica'=4,'expert'=8] {'replica','expert'}, use_global_device_ids=true, to_apply=%region_8.9 | all-reduce | flops 2 | bytes 16 | tf_op jit(solution)/shard_map/psum | solution.py:121
  336.8 3.8 fusion.38
  340.6 1.7 fusion.2
  342.3 1.7 fusion.3
  344.1 3.0 fusion.4
  347.1 17.7 %all-gather.2.cloned.1.call-done = bf16[2,128,4096]{2,1,0:T(8,128)(2,1)} async-done(((bf16[2,128,1024]{2,1,0:T(8,128)(2,1)}), bf16[2,128,4096]{2,1,0:T(8,128)(2,1)}) %all-gather.2.cloned.1.call-update) | async-done | bytes 2097168 | tf_op jit(solution)/shard_map/all_gather | solution.py:123
  364.8 2.4 reduce_sum.46
  367.2 2.8 fusion
  370.1 3.4 reduce_sum.48
  373.4 3.0 fusion.1
  (27 shorter events, 9.3 us)
Async XLA Ops:
  7.2 109.1 %copy-start = (bf16[1,128,4096]{2,1,0:T(8,128)(2,1)S(1)}, bf16[1,128,4096]{2,1,0:T(8,128)(2,1)}, u32[]{:S(2)}) copy-start(bf16[1,128,4096]{2,1,0:T(8,128)(2,1)} %param.15) | copy-start | bytes 3145732
  11.5 51.1 %all-to-all-start = ((bf16[8,32,4096]{2,1,0:T(8,128)(2,1)}), bf16[8,32,4096]{2,1,0:T(8,128)(2,1)S(1)}, u32[]{:S(2)}, u32[]{:S(2)}) async-start(bf16[8,32,4096]{2,1,0:T(8,128)(2,1)} %reshape.289), calls=%async_computation | async-start | bytes 4194304 | tf_op jit(solution)/shard_map/all_to_all | solution.py:62
  64.2 52.1 %all-to-all-start.2 = ((bf16[8,32,4096]{2,1,0:T(8,128)(2,1)}), bf16[8,32,4096]{2,1,0:T(8,128)(2,1)}, u32[]{:S(2)}, u32[]{:S(2)}) async-start(bf16[8,32,4096]{2,1,0:T(8,128)(2,1)} %reshape.291), calls=%async_computation.2 | async-start | bytes 4194304 | tf_op jit(solution)/shard_map/all_to_all | solution.py:87
  71.7 2.0 copy-start.1
  121.2 97.1 %all-to-all-start.1 = ((f32[8,32,4096]{2,1,0:T(8,128)}), f32[8,32,4096]{2,1,0:T(8,128)}, u32[]{:S(2)}, u32[]{:S(2)}) async-start(f32[8,32,4096]{2,1,0:T(8,128)} %fusion.7), calls=%async_computation.1 | async-start | bytes 8388608 | tf_op jit(solution)/shard_map/all_to_all | solution.py:77
  129.0 97.2 %reduce-scatter.2.cloned.1.call-start = ((), (), s32[]{:S(2)}) async-start(), calls=%async_computation.5 | async-start | bytes 2621440 | tf_op jit(solution)/shard_map/reduce_scatter | solution.py:117
  129.8 2.0 copy-start.2
  218.3 151.7 %all-to-all-start.3 = ((f32[8,32,4096]{2,1,0:T(8,128)}), f32[8,32,4096]{2,1,0:T(8,128)}, u32[]{:S(2)}, u32[]{:S(2)}) async-start(f32[8,32,4096]{2,1,0:T(8,128)} %bitcast.60), calls=%async_computation.3 | async-start | bytes 8388608 | tf_op jit(solution)/shard_map/all_to_all | solution.py:110
  226.2 138.6 %all-gather.2.cloned.1.call-start = ((), (), s32[]{:S(2)}) async-start(), calls=%async_computation.6 | async-start | bytes 2621440 | tf_op jit(solution)/shard_map/all_gather | solution.py:123
  370.0 6.4 %copy-start.3 = (bf16[2,128,4096]{2,1,0:T(8,128)(2,1)S(1)}, bf16[2,128,4096]{2,1,0:T(8,128)(2,1)}, u32[]{:S(2)}) copy-start(bf16[2,128,4096]{2,1,0:T(8,128)(2,1)} %all-gather.2.cloned.1.call-done) | copy-start | bytes 6291460
Sparse Core Ops, SparseCore 0:
  132.4 32.3 reduce-scatter.1
  340.7 24.0 all-gather.1
where the time goes:
time: 387 us; the launch traced here: 385 us
  waiting for transfers between devices  187 us (48%)
  blocking collectives  109 us (28%)
  starting transfers between devices  29.4 us (8%)
  matrix products  28.4 us (7%)
  between operations  14.1 us (4%)
  other arithmetic  12.5 us (3%)
  local copies, waits for them, and re-layouts  4.57 us (1%)
    psum x1, blocking collectives, body(): lax.psum(jnp.sum(pseudo * pseudo, axis=(1, 2)), ('replica', 'expert'))  109 us
    all_to_all x1, waiting for transfers between devices, body(): lax.all_to_all(partial_out, 'expert', split_axis=0, concat_axis=0, tiled=...  83.8 us
    all_to_all x1, waiting for transfers between devices, body(): lax.all_to_all(outbound, 'expert', split_axis=0, concat_axis=0, tiled=True)  43.3 us
    all_to_all x1, waiting for transfers between devices, body(): lax.all_to_all(outbound_dy, 'expert', split_axis=0, concat_axis=0, tiled=...  41.2 us
    all_gather x1, waiting for transfers between devices, body(): lax.all_gather(new_global.astype(jnp.bfloat16), 'replica', axis=2, tiled=...  17.7 us
    all_to_all x1, starting transfers between devices, body(): lax.all_to_all(partial_dx, 'expert', split_axis=0, concat_axis=0, tiled=T...  7.88 us
    all_to_all x1, starting transfers between devices, body(): lax.all_to_all(partial_out, 'expert', split_axis=0, concat_axis=0, tiled=...  7.82 us
  transfers between devices with their start and end apart: 6, of which 4 were waited for; matrix products, arithmetic and copies ran while one was open for 7% of the time, Pallas kernels for 0%

commit v1 on v0

--- a/solution.py
+++ b/solution.py
@@ -1,6 +1,10 @@
+import functools
+
 import jax
 import jax.numpy as jnp
 from jax import lax
+from jax.experimental import pallas as pl
+from jax.experimental.pallas import tpu as pltpu
 from jax.sharding import PartitionSpec as P
 
 D = 4096
@@ -28,7 +32,7 @@
     return (moment_next, anchor_next)
 
 
-def body(
+def general_body(
     tokens, routes, cweights, w_gate, w_up, w_down, grad_out, frag_local, frag_global, frag_moment
 ):
     groups = lax.axis_size("expert")
@@ -133,6 +137,659 @@
     )
 
 
+MESH = pl.DeviceIdType.MESH
+INNER = 2
+COLS = 512
+NT = (((1,), (1,)), ((), ()))
+TN = (((0,), (0,)), ((), ()))
+
+
+def step_kernel(
+    groups,
+    replicas,
+    x_ref,
+    dy_ref,
+    share_ref,
+    wg_ref,
+    wu_ref,
+    wd_ref,
+    fl_ref,
+    fg_ref,
+    fm_ref,
+    rows_ref,
+    dx_ref,
+    gg_ref,
+    gu_ref,
+    gd_ref,
+    ng_ref,
+    nm_ref,
+    nl_ref,
+    xs,
+    ys,
+    part,
+    part_dx,
+    from_pair,
+    from_left,
+    from_right,
+    wgu,
+    wd,
+    pre,
+    hid,
+    act_t,
+    dpre,
+    ggu,
+    gdn,
+    pieces,
+    fg,
+    fm,
+    pseudo,
+    fresh,
+    sq_part,
+    sq_exp,
+    sq_rep,
+    load_sem,
+    store_sem,
+    gather_send,
+    gather_recv,
+    gpair_send,
+    gpair_recv,
+    red_send,
+    red_recv,
+    rpair_send,
+    rpair_recv,
+    frag_send,
+    frag_recv,
+    frag_own_sem,
+    sqe_send,
+    sqe_recv,
+    sqr_send,
+    sqr_recv,
+    new_send,
+    new_recv,
+    new_own_sem,
+):
+    rep = lax.axis_index("replica")
+    me = lax.axis_index("expert")
+    outer = groups // INNER
+    z = me // INNER
+    y = me % INNER
+    pair = z * INNER + (1 - y)
+    width = x_ref.shape[1]
+    hidden = wd_ref.shape[0]
+    share_cols = fg_ref.shape[2]
+    frags = fg_ref.shape[0]
+    frag_rows = fg_ref.shape[1]
+
+    loads = [
+        pltpu.make_async_copy(wg_ref, wgu.at[:, pl.ds(0, hidden)], load_sem.at[0]),
+        pltpu.make_async_copy(wu_ref, wgu.at[:, pl.ds(hidden, hidden)], load_sem.at[1]),
+        pltpu.make_async_copy(wd_ref, wd, load_sem.at[2]),
+        pltpu.make_async_copy(fg_ref, fg, load_sem.at[3]),
+        pltpu.make_async_copy(fm_ref, fm, load_sem.at[4]),
+    ]
+    for load in loads:
+        load.start()
+
+    barrier = pltpu.get_barrier_semaphore()
+    for j in range(1, groups):
+        pl.semaphore_signal(
+            barrier, inc=1, device_id=(rep, lax.rem(me + j, groups)), device_id_type=MESH
+        )
+    for j in range(1, replicas):
+        pl.semaphore_signal(
+            barrier, inc=1, device_id=(lax.rem(rep + j, replicas), me), device_id_type=MESH
+        )
+    pl.semaphore_wait(barrier, groups - 1 + replicas - 1)
+
+    def block(z_of, y_of):
+        return pl.ds(pl.multiple_of((z_of * INNER + y_of) * CAP, CAP), CAP)
+
+    def remote(src, dst, send, recv, target):
+        return pltpu.make_async_remote_copy(
+            src_ref=src,
+            dst_ref=dst,
+            send_sem=send,
+            recv_sem=recv,
+            device_id=target,
+            device_id_type=MESH,
+        )
+
+    def right():
+        return (rep, jnp.minimum(z + 1, outer - 1) * INNER + y)
+
+    def left():
+        return (rep, jnp.maximum(z - 1, 0) * INNER + y)
+
+    def gather_copy(buf, which, way, hop, z_src):
+        rows = buf.at[block(z_src, y)]
+        return remote(
+            rows,
+            rows,
+            gather_send.at[which, way, hop],
+            gather_recv.at[which, way, hop],
+            right() if way == 0 else left(),
+        )
+
+    def gather_pair(buf, which, z_src, y_src):
+        rows = buf.at[block(z_src, y_src)]
+        return remote(
+            rows, rows, gpair_send.at[which, z_src], gpair_recv.at[which, z_src], (rep, pair)
+        )
+
+    def gather_step(buf, which, hop):
+        if hop == 0:
+
+            @pl.when(z < outer - 1)
+            def _():
+                gather_copy(buf, which, 0, 0, z).start()
+
+            @pl.when(z > 0)
+            def _():
+                gather_copy(buf, which, 1, 0, z).start()
+
+            gather_pair(buf, which, z, y).start()
+            return
+
+        @pl.when(z >= hop)
+        def _():
+            gather_copy(buf, which, 0, hop - 1, z - hop).wait_recv()
+
+            if hop < outer - 1:
+
+                @pl.when(z < outer - 1)
+                def _():
+                    gather_copy(buf, which, 0, hop, z - hop).start()
+
+            gather_pair(buf, which, z - hop, y).start()
+
+        @pl.when(z + hop < outer)
+        def _():
+            gather_copy(buf, which, 1, hop - 1, z + hop).wait_recv()
+
+            if hop < outer - 1:
+
+                @pl.when(z > 0)
+                def _():
+                    gather_copy(buf, which, 1, hop, z + hop).start()
+
+            gather_pair(buf, which, z + hop, y).start()
+
+    def gather_finish(buf, which):
+        for z_src in range(outer):
+            gather_pair(buf, which, z_src, 1 - y).wait_recv()
+
+    def gather_drain(buf, which):
+        for hop in range(outer - 1):
+
+            @pl.when((z < outer - 1) & (z >= hop))
+            def _():
+                gather_copy(buf, which, 0, hop, z - hop).wait_send()
+
+            @pl.when((z > 0) & (z + hop < outer))
+            def _():
+                gather_copy(buf, which, 1, hop, z + hop).wait_send()
+
+        for z_src in range(outer):
+            gather_pair(buf, which, z_src, y).wait_send()
+
+    order = []
+    for k in range(outer // 2):
+        order += [outer - 1 - k, k]
+    if outer % 2:
+        order.append(outer // 2)
+
+    def reduce_pair(buf, which, z_dst):
+        return remote(
+            buf.at[block(z_dst, 1 - y)],
+            from_pair.at[which, z_dst],
+            rpair_send.at[which, z_dst],
+            rpair_recv.at[which, z_dst],
+            (rep, pair),
+        )
+
+    def reduce_line(buf, which, way, z_dst):
+        landing = from_left if way == 0 else from_right
+        return remote(
+            buf.at[block(z_dst, y)],
+            landing.at[which, z_dst],
+            red_send.at[which, way, z_dst],
+            red_recv.at[which, way, z_dst],
+            right() if way == 0 else left(),
+        )
+
+    def reduce_start(buf, which):
+        for z_dst in order:
+            reduce_pair(buf, which, z_dst).start()
+
+    def add_in(buf, z_dst, landed):
+        rows = block(z_dst, y)
+        buf[rows, :] = (
+            buf[rows, :].astype(jnp.float32) + landed.astype(jnp.float32)
+        ).astype(jnp.bfloat16)
+
+    def add_two(buf, z_dst, first, second):
+        rows = block(z_dst, y)
+        buf[rows, :] = (
+            buf[rows, :].astype(jnp.float32)
+            + first.astype(jnp.float32)
+            + second.astype(jnp.float32)
+        ).astype(jnp.bfloat16)
+
+    def reduce_step(buf, which, k):
+        z_dst = order[k]
+        reduce_pair(buf, which, z_dst).wait_recv()
+
+        @pl.when(z < z_dst)
+        def _():
+            @pl.when(z > 0)
+            def _():
+                reduce_line(buf, which, 0, z_dst).wait_recv()
+                add_two(buf, z_dst, from_pair[which, z_dst], from_left[which, z_dst])
+
+            @pl.when(z == 0)
+            def _():
+                add_in(buf, z_dst, from_pair[which, z_dst])
+
+            reduce_line(buf, which, 0, z_dst).start()
+
+        @pl.when(z > z_dst)
+        def _():
+            @pl.when(z < outer - 1)
+            def _():
+                reduce_line(buf, which, 1, z_dst).wait_recv()
+                add_two(buf, z_dst, from_pair[which, z_dst], from_right[which, z_dst])
+
+            @pl.when(z == outer - 1)
+            def _():
+                add_in(buf, z_dst, from_pair[which, z_dst])
+
+            reduce_line(buf, which, 1, z_dst).start()
+
+    def reduce_finish(buf, which, total):
+        total[...] = buf[block(z, y), :].astype(jnp.float32) + from_pair[which, z].astype(
+            jnp.float32
+        )
+
+        @pl.when(z > 0)
+        def _():
+            reduce_line(buf, which, 0, z).wait_recv()
+            total[...] += from_left[which, z].astype(jnp.float32)
+
+        @pl.when(z < outer - 1)
+        def _():
+            reduce_line(buf, which, 1, z).wait_recv()
+            total[...] += from_right[which, z].astype(jnp.float32)
+
+    def reduce_drain(buf, which):
+        for z_dst in range(outer):
+            reduce_pair(buf, which, z_dst).wait_send()
+
+            @pl.when(z < z_dst)
+            def _():
+                reduce_line(buf, which, 0, z_dst).wait_send()
+
+            @pl.when(z > z_dst)
+            def _():
+                reduce_line(buf, which, 1, z_dst).wait_send()
+
+    def columns(index):
+        return pl.ds(pl.multiple_of(index * share_cols, share_cols), share_cols)
+
+    def frag_copy(j):
+        target = lax.rem(rep + j, replicas)
+        return remote(
+            fl_ref.at[:, :, columns(target)],
+            pieces.at[j],
+            frag_send.at[j],
+            frag_recv.at[j],
+            (target, me),
+        )
+
+    def new_copy(j):
+        return remote(
+            fresh,
+            nl_ref.at[:, :, columns(rep)],
+            new_send.at[j],
+            new_recv.at[j],
+            (lax.rem(rep + j, replicas), me),
+        )
+
+    def new_arrival(j):
+        return remote(
+            fresh,
+            nl_ref.at[:, :, columns(lax.rem(rep + replicas - j, replicas))],
+            new_send.at[j],
+            new_recv.at[j],
+            (lax.rem(rep + j, replicas), me),
+        )
+
+    def sqe_copy(j):
+        return remote(
+            sq_part.at[0],
+            sq_exp.at[j],
+            sqe_send.at[j],
+            sqe_recv.at[j],
+            (rep, lax.rem(me + j, groups)),
+        )
+
+    def sqr_copy(j):
+        return remote(
+            sq_part.at[1],
+            sq_rep.at[j],
+            sqr_send.at[j],
+            sqr_recv.at[j],
+            (lax.rem(rep + j, replicas), me),
+        )
+
+    mine = block(z, y)
+    xs[mine, :] = x_ref[...]
+    gather_step(xs, 0, 0)
+    frag_order = [replicas // 2] + [j for j in range(1, replicas) if j != replicas // 2]
+    for j in frag_order:
+        frag_copy(j).start()
+    own_piece = pltpu.make_async_copy(fl_ref.at[:, :, columns(rep)], pieces.at[0], frag_own_sem)
+    own_piece.start()
+    ys[mine, :] = dy_ref[...]
+    for hop in range(1, outer - 1):
+        gather_step(xs, 0, hop)
+    gather_step(ys, 1, 0)
+    gather_step(xs, 0, outer - 1)
+    loads[0].wait()
+    loads[1].wait()
+    gather_finish(xs, 0)
+
+    tiles = width // COLS
+
+    def tile(index):
+        return pl.ds(pl.multiple_of(index * COLS, COLS), COLS)
+
+    pre[...] = jnp.zeros_like(pre)
+
+    @pl.loop(0, tiles)
+    def _(t):
+        pre[...] += jnp.dot(xs[:, tile(t)], wgu[tile(t), :], preferred_element_type=jnp.float32)
+
+    gate_pre = pre[:, :hidden]
+    silu_val, _ = silu_parts(gate_pre)
+    act = (silu_val * pre[:, hidden:]).astype(jnp.bfloat16)
+    hid[...] = act
+    act_t[...] = act.astype(jnp.float32).T.astype(jnp.bfloat16)
+    loads[2].wait()
+
+    @pl.loop(0, tiles)
+    def _(t):
+        part[:, tile(t)] = jnp.dot(
+            hid[...], wd[:, tile(t)], preferred_element_type=jnp.float32
+        ).astype(jnp.bfloat16)
+
+    reduce_start(part, 0)
+    gather_step(ys, 1, 1)
+
+    loads[3].wait()
+    own_piece.wait()
+    for j in range(1, replicas):
+        frag_copy(j).wait_recv()
+    chunk = 32 if frag_rows % 32 == 0 else 16
+    lanes = []
+    for f in range(frags):
+
+        def accumulate(i, total, f=f):
+            rows = pl.ds(pl.multiple_of(i * chunk, chunk), chunk)
+            summed = pieces[0, f, rows, :].astype(jnp.float32)
+            for j in range(1, replicas):
+                summed += pieces[j, f, rows, :].astype(jnp.float32)
+            value = fg[f, rows, :] - summed * (1.0 / replicas)
+            pseudo[f, rows, :] = value
+            return total + jnp.sum(value * value, axis=0, keepdims=True)
+
+        total = lax.fori_loop(
+            0, frag_rows // chunk, accumulate, jnp.zeros((1, share_cols), jnp.float32)
+        )
+        lanes.append(jnp.sum(total, axis=1, keepdims=True))
+    row_ids = lax.broadcasted_iota(jnp.int32, (8, 128), 0)
+    tile_sum = jnp.zeros((8, 128), jnp.float32)
+    for f in range(frags):
+        tile_sum = jnp.where(row_ids == f, lanes[f], tile_sum)
+    sq_part[0] = tile_sum
+    for j in range(1, groups):
+        sqe_copy(j).start()
+
+    reduce_step(part, 0, 0)
+    gather_step(ys, 1, 2)
+    reduce_step(part, 0, 1)
+    for hop in range(3, outer):
+        gather_step(ys, 1, hop)
+
+    for j in range(1, groups):
+        sqe_copy(j).wait_recv()
+    over_experts = sq_part[0]
+    for j in range(1, groups):
+        over_experts += sq_exp[j]
+    sq_part[1] = over_experts
+    for j in range(1, replicas):
+        sqr_copy(j).start()
+    for k in range(2, outer):
+        reduce_step(part, 0, k)
+    gather_finish(ys, 1)
+
+    pre_dact = ggu.at[0]
+    pre_dact[...] = jnp.zeros_like(pre_dact)
+
+    @pl.loop(0, tiles)
+    def _(t):
+        pre_dact[...] += lax.dot_general(
+            ys[:, tile(t)], wd[:, tile(t)], NT, preferred_element_type=jnp.float32
+        )
+
+    grad_hidden = pre_dact[...]
+    silu_val, silu_slope = silu_parts(pre[:, :hidden])
+    dpre[:, :hidden] = (grad_hidden * pre[:, hidden:] * silu_slope).astype(jnp.bfloat16)
+    dpre[:, hidden:] = (grad_hidden * silu_val).astype(jnp.bfloat16)
+
+    @pl.loop(0, tiles)
+    def _(t):
+        part_dx[:, tile(t)] = lax.dot_general(
+            dpre[...], wgu[tile(t), :], NT, preferred_element_type=jnp.float32
+        ).astype(jnp.bfloat16)
+
+    reduce_start(part_dx, 1)
+
+    loads[4].wait()
+    for j in range(1, replicas):
+        sqr_copy(j).wait_recv()
+    squares = sq_part[1]
+    for j in range(1, replicas):
+        squares += sq_rep[j]
+    limit = CLIP_RMS * (HID * D) ** 0.5
+    factors = jnp.minimum(jnp.float32(1.0), limit / (jnp.sqrt(squares) + 1e-06))
+    for f in range(frags):
+        factor = factors[f : f + 1, :1]
+
+        def update(i, carry, f=f, factor=factor):
+            rows = pl.ds(pl.multiple_of(i * chunk, chunk), chunk)
+            clipped = pseudo[f, rows, :] * factor
+            moment = OUTER_MOMENTUM * fm[f, rows, :] + clipped
+            anchor = fg[f, rows, :] - OUTER_RATE * (OUTER_MOMENTUM * moment + clipped)
+            fm[f, rows, :] = moment
+            fg[f, rows, :] = anchor
+            fresh[f, rows, :] = anchor.astype(jnp.bfloat16)
+            return carry
+
+        lax.fori_loop(0, frag_rows // chunk, update, 0)
+    for j in frag_order:
+        new_copy(j).start()
+    own_new = pltpu.make_async_copy(fresh, nl_ref.at[:, :, columns(rep)], new_own_sem)
+    own_new.start()
+    stores = [
+        pltpu.make_async_copy(fg, ng_ref, store_sem.at[0]),
+        pltpu.make_async_copy(fm, nm_ref, store_sem.at[1]),
+    ]
+    for store in stores:
+        store.start()
+
+    reduce_finish(part, 0, rows_ref)
+    rows_ref[...] = rows_ref[...] * share_ref[...]
+    reduce_step(part_dx, 1, 0)
+    reduce_step(part_dx, 1, 1)
+
+    @pl.loop(0, tiles)
+    def _(t):
+        both = lax.dot_general(
+            xs[:, tile(t)], dpre[...], TN, preferred_element_type=jnp.float32
+        ).astype(jnp.bfloat16)
+        gdn[0, tile(t), :] = both[:, :hidden]
+        gdn[1, tile(t), :] = both[:, hidden:]
+
+    more = [
+        pltpu.make_async_copy(gdn.at[0], gg_ref, store_sem.at[2]),
+        pltpu.make_async_copy(gdn.at[1], gu_ref, store_sem.at[3]),
+    ]
+    for store in more:
+        store.start()
+    for k in range(2, outer):
+        reduce_step(part_dx, 1, k)
+    gd_out = wd
+
+    @pl.loop(0, tiles)
+    def _(t):
+        gd_out[:, tile(t)] = jnp.dot(
+            act_t[...], ys[:, tile(t)], preferred_element_type=jnp.float32
+        ).astype(jnp.bfloat16)
+
+    last = pltpu.make_async_copy(gd_out, gd_ref, store_sem.at[4])
+    last.start()
+
+    reduce_finish(part_dx, 1, dx_ref)
+
+    for buf, which in ((xs, 0), (ys, 1)):
+        gather_drain(buf, which)
+    for buf, which in ((part, 0), (part_dx, 1)):
+        reduce_drain(buf, which)
+    for j in range(1, groups):
+        sqe_copy(j).wait_send()
+    for j in range(1, replicas):
+        frag_copy(j).wait_send()
+        sqr_copy(j).wait_send()
+        new_copy(j).wait_send()
+        new_arrival(j).wait_recv()
+    own_new.wait()
+    for store in stores + more + [last]:
+        store.wait()
+
+
+def pair_body(
+    tokens, routes, cweights, w_gate, w_up, w_down, grad_out, frag_local, frag_global, frag_moment
+):
+    groups = lax.axis_size("expert")
+    replicas = lax.axis_size("replica")
+    inputs, grads_in = tokens[0], grad_out[0]
+    width = inputs.shape[1]
+    hidden = w_down.shape[1]
+    frags, frag_rows, cols = frag_global.shape
+    matched = routes[0] == 0
+    routed = jnp.any(matched, axis=1)
+    share = jnp.sum(jnp.where(matched, cweights[0], jnp.float32(0.0)), axis=1)
+    ahead = jnp.arange(routed.shape[0], dtype=jnp.int32)
+    earlier = (ahead[None, :] <= ahead[:, None]) & routed[None, :]
+    places = jnp.sum(earlier.astype(jnp.int32), axis=1) - 1
+    slot_ids = jnp.arange(CAP, dtype=jnp.int32)
+    layout = routed[None, :] & (places[None, :] == slot_ids[:, None])
+    layout_b = layout.astype(jnp.bfloat16)
+    slot_share = jnp.sum(jnp.where(layout, share[None, :], 0.0), axis=1, keepdims=True)
+    picked = jnp.dot(layout_b, inputs, preferred_element_type=jnp.float32).astype(jnp.bfloat16)
+    dy = jnp.dot(layout_b, grads_in, preferred_element_type=jnp.float32)
+    dy = (dy * slot_share).astype(jnp.bfloat16)
+    bf, f32 = jnp.bfloat16, jnp.float32
+    outer = groups // INNER
+    total = groups * CAP
+    dma = pltpu.SemaphoreType.DMA
+    vmem, hbm = pl.BlockSpec(memory_space=pltpu.VMEM), pl.BlockSpec(memory_space=pl.ANY)
+    shape = jax.ShapeDtypeStruct
+    rows, dx, gg, gu, gd, ng, nm, nl = pl.pallas_call(
+        functools.partial(step_kernel, groups, replicas),
+        out_shape=(
+            shape((CAP, width), f32),
+            shape((CAP, width), f32),
+            shape((width, hidden), bf),
+            shape((width, hidden), bf),
+            shape((hidden, width), bf),
+            shape(frag_global.shape, f32),
+            shape(frag_global.shape, f32),
+            shape(frag_local.shape[1:], bf),
+        ),
+        in_specs=[vmem] * 3 + [hbm] * 6,
+        out_specs=(vmem,) * 2 + (hbm,) * 6,
+        scratch_shapes=[
+            pltpu.VMEM((total, width), bf),
+            pltpu.VMEM((total, width), bf),
+            pltpu.VMEM((total, width), bf),
+            pltpu.VMEM((total, width), bf),
+            pltpu.VMEM((2, outer, CAP, width), bf),
+            pltpu.VMEM((2, outer, CAP, width), bf),
+            pltpu.VMEM((2, outer, CAP, width), bf),
+            pltpu.VMEM((width, 2 * hidden), bf),
+            pltpu.VMEM((hidden, width), bf),
+            pltpu.VMEM((total, 2 * hidden), f32),
+            pltpu.VMEM((total, hidden), bf),
+            pltpu.VMEM((hidden, total), bf),
+            pltpu.VMEM((total, 2 * hidden), bf),
+            pltpu.VMEM((1, total, hidden), f32),
+            pltpu.VMEM((2, width, hidden), bf),
+            pltpu.VMEM((replicas, frags, frag_rows, cols), bf),
+            pltpu.VMEM(frag_global.shape, f32),
+            pltpu.VMEM(frag_global.shape, f32),
+            pltpu.VMEM(frag_global.shape, f32),
+            pltpu.VMEM(frag_global.shape, bf),
+            pltpu.VMEM((2, 8, 128), f32),
+            pltpu.VMEM((groups, 8, 128), f32),
+            pltpu.VMEM((replicas, 8, 128), f32),
+            dma((5,)),
+            dma((5,)),
+            dma((2, 2, outer)),
+            dma((2, 2, outer)),
+            dma((2, outer)),
+            dma((2, outer)),
+            dma((2, 2, outer)),
+            dma((2, 2, outer)),
+            dma((2, outer)),
+            dma((2, outer)),
+            dma((replicas,)),
+            dma((replicas,)),
+            dma,
+            dma((groups,)),
+            dma((groups,)),
+            dma((replicas,)),
+            dma((replicas,)),
+            dma((replicas,)),
+            dma((replicas,)),
+            dma,
+        ],
+        compiler_params=pltpu.CompilerParams(
+            collective_id=0, has_side_effects=True, vmem_limit_bytes=56 * 2**20
+        ),
+    )(
+        picked,
+        dy,
+        slot_share,
+        w_gate[0],
+        w_up[0],
+        w_down[0],
+        frag_local[0],
+        frag_global,
+        frag_moment,
+    )
+    back = layout_b.T
+    layer_out = jnp.dot(back, rows.astype(bf), preferred_element_type=f32).astype(bf)
+    grad_tokens = jnp.dot(back, dx.astype(bf), preferred_element_type=f32).astype(bf)
+    return (layer_out[None], grad_tokens[None], gg[None], gu[None], gd[None], ng, nm, nl[None])
+
+
+def body(*operands):
+    if lax.axis_size("expert") == SPLIT:
+        return pair_body(*operands)
+    return general_body(*operands)
+
+
 def solution(mesh):
     return jax.shard_map(
         body,

time: 387 us -> 137 us (0.35)
  waiting for transfers between devices: 187 us -> 0 us
  Pallas kernels: 0 us -> 118 us
  blocking collectives: 109 us -> 0 us
  starting transfers between devices: 29.4 us -> 0 us
  matrix products: 28.4 us -> 8.34 us
  between operations: 14.1 us -> 0.69 us
  other arithmetic: 12.5 us -> 1.05 us
    all_to_all x4 -> x0, waiting for transfers between devices: 168 us -> none  [the longest x1 83.8 us: body(): lax.all_to_all(partial_out, 'expert', split_axis=0, concat_axis=0, tiled=...]
    pallas_call x0 -> x1, Pallas kernels: none -> 118 us  [pair_body(): pl.pallas_call(functools.partial(step_kernel, groups, replicas), out_shap...]
    psum x1 -> x0, blocking collectives: 109 us -> none  [body(): lax.psum(jnp.sum(pseudo * pseudo, axis=(1, 2)), ('replica', 'expert'))]
    all_to_all x4 -> x0, starting transfers between devices: 29.4 us -> none  [the longest x1 7.88 us: body(): lax.all_to_all(partial_dx, 'expert', split_axis=0, concat_axis=0, tiled=T...]
    dot_general x13 -> x4, matrix products: 28.4 us -> 8.34 us  [the longest x1 2.58 us: pair_body(): jnp.dot(back, dx.astype(bf), preferred_element_type=f32).astype(bf)]
    all_gather x1 -> x0, waiting for transfers between devices: 17.7 us -> none  [body(): lax.all_gather(new_global.astype(jnp.bfloat16), 'replica', axis=2, tiled=...]
    reduce_sum x5 -> x3, other arithmetic: 8.41 us -> 1.03 us  [the longest x1 0.81 us: pair_body(): share = jnp.sum(jnp.where(matched, cweights[0], jnp.float32(0.0)), axis=1)]
    unnamed x9 -> x20, local copies, waits for them, and re-layouts: 1.34 us -> 6.53 us
  transfers between devices with their start and end apart: 6 -> 0, of which waited for: 4 -> 0; matrix products, arithmetic and copies ran while one was open for 7% -> 0% of each run, Pallas kernels for 0% -> 0%
where the time goes in v1:
time: 137 us; the launch traced here: 136 us
  Pallas kernels  118 us (86%)
  matrix products  8.34 us (6%)
  local copies, waits for them, and re-layouts  7.22 us (5%)
    pallas_call x1, Pallas kernels, pair_body(): pl.pallas_call(functools.partial(step_kernel, groups, replicas), out_shap...  118 us
    unnamed x20, local copies, waits for them, and re-layouts  6.53 us

profile of v1, /device:TPU:16, one launch (start us, length us, event | category | flops | bytes accessed | tf_op | source)
XLA Modules:
  0.0 135.7 jit_solution(6786913855137053685)
XLA Ops:
  0.6 0.0 copy-start
  0.6 0.8 select_reduce_fusion.1
  1.5 0.1 convert_reduce_fusion
  1.6 0.1 select_reduce_fusion
  1.7 0.2 copy-done
  1.9 1.0 fusion.2.dy_ref
  2.9 0.7 copy.19.share_ref
  3.6 2.2 %convolution_convert_fusion.2.x_ref = bf16[32,4096]{1,0:T(8,128)(2,1)} fusion(bf16[1,128,4096]{2,1,0:T(8,128)(2,1)} %param.10, s32[128]{0:T(128)S(1)} %broadcast_add_fusion, pred[128]{0:T(512)(128)(4,1)S(1)} %reduce_or.9), kind=kOutput, calls=%fused_computation.6 | convolution fusion | flops 33693696 | bytes 1311360 | tf_op jit(solution)/shard_map/dot_general | solution.py:699
  5.8 118.4 %shard_map.161 = (f32[32,4096]{1,0:T(8,128)}, f32[32,4096]{1,0:T(8,128)}, bf16[4096,128]{1,0:T(8,128)(2,1)}, bf16[4096,128]{1,0:T(8,128)(2,1)}, bf16[128,4096]{1...) custom-call(bf16[32,4096]{1,0:T(8,128)(2,1)} %convolution_convert_fusion.2.x_ref, ...), custom_call_target="tpu_custom_call" | custom-call | tf_op jit(solution)/shard_map/pallas_call | solution.py:708
  124.2 0.0 copy-start.6
  124.2 2.6 %fusion.1 = bf16[1,128,4096]{2,1,0:T(8,128)(2,1)} fusion(f32[32,4096]{1,0:T(8,128)} %get-tuple-element.17, s32[128]{0:T(128)S(1)} %broadcast_add_fusion, pred[128]{0:T(512)(128)(4,1)S(1)} %reduce_or.9), kind=kOutput, calls=%fused_computation.3 | convolution fusion | flops 34217984 | bytes 1573504 | tf_op jit(solution)/shard_map/dot_general | solution.py:783
  126.8 2.6 %fusion = bf16[1,128,4096]{2,1,0:T(8,128)(2,1)} fusion(f32[32,4096]{1,0:T(8,128)} %get-tuple-element.16, s32[128]{0:T(128)S(1)} %broadcast_add_fusion, pred[128]{0:T(512)(128)(4,1)S(1)} %reduce_or.9), kind=kOutput, calls=%fused_computation.2 | convolution fusion | flops 34217984 | bytes 1573504 | tf_op jit(solution)/shard_map/dot_general | solution.py:782
  129.3 0.0 copy-done.6
  129.3 1.0 copy.26
  130.3 0.0 copy-done.5
  130.3 1.0 copy.27
  131.3 0.0 copy-done.4
  131.3 1.0 copy.28
  132.3 0.0 copy-done.3
  132.3 1.0 copy.29
  133.2 0.0 copy-done.2
  133.2 1.0 copy.30
  134.2 0.1 copy-done.1
  134.4 1.3 copy.31
  (7 shorter events, 0.0 us)
Async XLA Ops:
  0.6 1.3 copy-start
  124.2 5.2 %copy-start.6 = (bf16[4096,128]{1,0:T(8,128)(2,1)S(1)}, bf16[4096,128]{1,0:T(8,128)(2,1)}, u32[]{:S(2)}) copy-start(bf16[4096,128]{1,0:T(8,128)(2,1)} %get-tuple-element.18) | copy-start | bytes 3145732
  126.8 3.6 %copy-start.5 = (bf16[4096,128]{1,0:T(8,128)(2,1)S(1)}, bf16[4096,128]{1,0:T(8,128)(2,1)}, u32[]{:S(2)}) copy-start(bf16[4096,128]{1,0:T(8,128)(2,1)} %get-tuple-element.19) | copy-start | bytes 3145732
  129.3 1.9 %copy-start.4 = (bf16[128,4096]{1,0:T(8,128)(2,1)S(1)}, bf16[128,4096]{1,0:T(8,128)(2,1)}, u32[]{:S(2)}) copy-start(bf16[128,4096]{1,0:T(8,128)(2,1)} %get-tuple-element.20) | copy-start | bytes 3145732
  130.3 1.9 %copy-start.3 = (f32[2,128,1024]{2,1,0:T(8,128)S(1)}, f32[2,128,1024]{2,1,0:T(8,128)}, u32[]{:S(2)}) copy-start(f32[2,128,1024]{2,1,0:T(8,128)} %get-tuple-element.39) | copy-start | bytes 3145732
  131.3 1.9 %copy-start.2 = (f32[2,128,1024]{2,1,0:T(8,128)S(1)}, f32[2,128,1024]{2,1,0:T(8,128)}, u32[]{:S(2)}) copy-start(f32[2,128,1024]{2,1,0:T(8,128)} %get-tuple-element.40) | copy-start | bytes 3145732
  132.3 2.1 %copy-start.1 = (bf16[2,128,4096]{2,1,0:T(8,128)(2,1)S(1)}, bf16[2,128,4096]{2,1,0:T(8,128)(2,1)}, u32[]{:S(2)}) copy-start(bf16[2,128,4096]{2,1,0:T(8,128)(2,1)} %get-tuple-element.23) | copy-start | bytes 6291460

commit v2 on v1

--- a/solution.py
+++ b/solution.py
@@ -140,6 +140,7 @@
 MESH = pl.DeviceIdType.MESH
 INNER = 2
 COLS = 512
+SPLITS = ((3584, 2560), (2560, 3584))
 NT = (((1,), (1,)), ((), ()))
 TN = (((0,), (0,)), ((), ()))
 
@@ -147,17 +148,19 @@
 def step_kernel(
     groups,
     replicas,
+    splits,
     x_ref,
+    routes_ref,
+    weights_ref,
     dy_ref,
-    share_ref,
     wg_ref,
     wu_ref,
     wd_ref,
     fl_ref,
     fg_ref,
     fm_ref,
-    rows_ref,
-    dx_ref,
+    lo_ref,
+    gt_ref,
     gg_ref,
     gu_ref,
     gd_ref,
@@ -187,6 +190,9 @@
     sq_part,
     sq_exp,
     sq_rep,
+    total,
+    placed,
+    grads,
     load_sem,
     store_sem,
     gather_send,
@@ -226,6 +232,7 @@
         pltpu.make_async_copy(wd_ref, wd, load_sem.at[2]),
         pltpu.make_async_copy(fg_ref, fg, load_sem.at[3]),
         pltpu.make_async_copy(fm_ref, fm, load_sem.at[4]),
+        pltpu.make_async_copy(dy_ref, grads, load_sem.at[5]),
     ]
     for load in loads:
         load.start()
@@ -239,8 +246,6 @@
         pl.semaphore_signal(
             barrier, inc=1, device_id=(lax.rem(rep + j, replicas), me), device_id_type=MESH
         )
-    pl.semaphore_wait(barrier, groups - 1 + replicas - 1)
-
     def block(z_of, y_of):
         return pl.ds(pl.multiple_of((z_of * INNER + y_of) * CAP, CAP), CAP)
 
@@ -260,77 +265,106 @@
     def left():
         return (rep, jnp.maximum(z - 1, 0) * INNER + y)
 
-    def gather_copy(buf, which, way, hop, z_src):
-        rows = buf.at[block(z_src, y)]
+    def near(which, gather):
+        return pl.ds(0, splits[gather][which])
+
+    def far(which, gather):
+        return pl.ds(splits[gather][which], width - splits[gather][which])
+
+    def toward(way):
+        return right() if way == 0 else left()
+
+    def other(stream):
+        return y if stream == 0 else 1 - y
+
+    def gather_copy(buf, which, way, hop, z_src, stream):
+        cols = near(which, 0) if stream == 2 else far(which, 0)
+        rows = buf.at[block(z_src, y if stream == 2 else other(stream)), cols]
         return remote(
             rows,
             rows,
-            gather_send.at[which, way, hop],
-            gather_recv.at[which, way, hop],
-            right() if way == 0 else left(),
+            gather_send.at[which, way, stream, hop],
+            gather_recv.at[which, way, stream, hop],
+            toward(way),
         )
 
     def gather_pair(buf, which, z_src, y_src):
-        rows = buf.at[block(z_src, y_src)]
+        rows = buf.at[block(z_src, y_src), near(which, 0)]
         return remote(
             rows, rows, gpair_send.at[which, z_src], gpair_recv.at[which, z_src], (rep, pair)
         )
 
+    def gather_swap(buf, which, y_src):
+        rows = buf.at[block(z, y_src), far(which, 0)]
+        return remote(
+            rows, rows, gpair_send.at[which, outer], gpair_recv.at[which, outer], (rep, pair)
+        )
+
+    def gather_both_ways(buf, which, stream):
+        @pl.when(z < outer - 1)
+        def _():
+            gather_copy(buf, which, 0, 0, z, stream).start()
+
+        @pl.when(z > 0)
+        def _():
+            gather_copy(buf, which, 1, 0, z, stream).start()
+
+    def gather_start(buf, which):
+        gather_swap(buf, which, y).start()
+        gather_both_ways(buf, which, 2)
+        gather_pair(buf, which, z, y).start()
+        gather_both_ways(buf, which, 0)
+
+    def gather_turn(buf, which):
+        gather_swap(buf, which, 1 - y).wait_recv()
+        gather_both_ways(buf, which, 1)
+
     def gather_step(buf, which, hop):
-        if hop == 0:
-
-            @pl.when(z < outer - 1)
-            def _():
-                gather_copy(buf, which, 0, 0, z).start()
-
-            @pl.when(z > 0)
-            def _():
-                gather_copy(buf, which, 1, 0, z).start()
-
-            gather_pair(buf, which, z, y).start()
-            return
-
-        @pl.when(z >= hop)
-        def _():
-            gather_copy(buf, which, 0, hop - 1, z - hop).wait_recv()
-
-            if hop < outer - 1:
-
-                @pl.when(z < outer - 1)
-                def _():
-                    gather_copy(buf, which, 0, hop, z - hop).start()
-
-            gather_pair(buf, which, z - hop, y).start()
-
-        @pl.when(z + hop < outer)
-        def _():
-            gather_copy(buf, which, 1, hop - 1, z + hop).wait_recv()
-
-            if hop < outer - 1:
-
-                @pl.when(z > 0)
-                def _():
-                    gather_copy(buf, which, 1, hop, z + hop).start()
-
-            gather_pair(buf, which, z + hop, y).start()
+        for stream in (2, 0, 1):
+
+            @pl.when(z >= hop)
+            def _(stream=stream):
+                gather_copy(buf, which, 0, hop - 1, z - hop, stream).wait_recv()
+                if hop < outer - 1:
+
+                    @pl.when(z < outer - 1)
+                    def _():
+                        gather_copy(buf, which, 0, hop, z - hop, stream).start()
+
+                if stream == 2:
+                    gather_pair(buf, which, z - hop, y).start()
+
+            @pl.when(z + hop < outer)
+            def _(stream=stream):
+                gather_copy(buf, which, 1, hop - 1, z + hop, stream).wait_recv()
+                if hop < outer - 1:
+
+                    @pl.when(z > 0)
+                    def _():
+                        gather_copy(buf, which, 1, hop, z + hop, stream).start()
+
+                if stream == 2:
+                    gather_pair(buf, which, z + hop, y).start()
 
     def gather_finish(buf, which):
         for z_src in range(outer):
             gather_pair(buf, which, z_src, 1 - y).wait_recv()
 
     def gather_drain(buf, which):
-        for hop in range(outer - 1):
-
-            @pl.when((z < outer - 1) & (z >= hop))
-            def _():
-                gather_copy(buf, which, 0, hop, z - hop).wait_send()
-
-            @pl.when((z > 0) & (z + hop < outer))
-            def _():
-                gather_copy(buf, which, 1, hop, z + hop).wait_send()
+        for stream in range(3):
+            for hop in range(outer - 1):
+
+                @pl.when((z < outer - 1) & (z >= hop))
+                def _(stream=stream, hop=hop):
+                    gather_copy(buf, which, 0, hop, z - hop, stream).wait_send()
+
+                @pl.when((z > 0) & (z + hop < outer))
+                def _(stream=stream, hop=hop):
+                    gather_copy(buf, which, 1, hop, z + hop, stream).wait_send()
 
         for z_src in range(outer):
             gather_pair(buf, which, z_src, y).wait_send()
+        gather_swap(buf, which, y).wait_send()
 
     order = []
     for k in range(outer // 2):
@@ -340,97 +374,125 @@
 
     def reduce_pair(buf, which, z_dst):
         return remote(
-            buf.at[block(z_dst, 1 - y)],
-            from_pair.at[which, z_dst],
+            buf.at[block(z_dst, 1 - y), near(which, 1)],
+            from_pair.at[which, z_dst, :, near(which, 1)],
             rpair_send.at[which, z_dst],
             rpair_recv.at[which, z_dst],
             (rep, pair),
         )
 
-    def reduce_line(buf, which, way, z_dst):
-        landing = from_left if way == 0 else from_right
-        return remote(
-            buf.at[block(z_dst, y)],
-            landing.at[which, z_dst],
-            red_send.at[which, way, z_dst],
-            red_recv.at[which, way, z_dst],
-            right() if way == 0 else left(),
+    def reduce_swap(buf, which):
+        return remote(
+            buf.at[block(z, 1 - y), far(which, 1)],
+            from_pair.at[which, z, :, far(which, 1)],
+            rpair_send.at[which, outer],
+            rpair_recv.at[which, outer],
+            (rep, pair),
+        )
+
+    def landing(which, way, z_dst, stream):
+        held = from_left if way == 0 else from_right
+        cols = near(which, 1) if stream == 2 else far(which, 1)
+        return held.at[which, 1 if stream == 1 else 0, z_dst, :, cols]
+
+    def home(buf, which, z_dst, stream):
+        cols = near(which, 1) if stream == 2 else far(which, 1)
+        return buf.at[block(z_dst, y if stream == 2 else other(stream)), cols]
+
+    def reduce_line(buf, which, way, z_dst, stream):
+        return remote(
+            home(buf, which, z_dst, stream),
+            landing(which, way, z_dst, stream),
+            red_send.at[which, way, stream, z_dst],
+            red_recv.at[which, way, stream, z_dst],
+            toward(way),
         )
 
     def reduce_start(buf, which):
         for z_dst in order:
             reduce_pair(buf, which, z_dst).start()
 
-    def add_in(buf, z_dst, landed):
-        rows = block(z_dst, y)
-        buf[rows, :] = (
-            buf[rows, :].astype(jnp.float32) + landed.astype(jnp.float32)
-        ).astype(jnp.bfloat16)
-
-    def add_two(buf, z_dst, first, second):
-        rows = block(z_dst, y)
-        buf[rows, :] = (
-            buf[rows, :].astype(jnp.float32)
-            + first.astype(jnp.float32)
-            + second.astype(jnp.float32)
-        ).astype(jnp.bfloat16)
-
-    def reduce_step(buf, which, k):
+    def add_to(target, *terms):
+        value = target[...].astype(jnp.float32)
+        for term in terms:
+            value = value + term[...].astype(jnp.float32)
+        target[...] = value.astype(jnp.bfloat16)
+
+    def reduce_step(buf, which, k, streams=(1, 0, 2)):
         z_dst = order[k]
-        reduce_pair(buf, which, z_dst).wait_recv()
-
-        @pl.when(z < z_dst)
-        def _():
-            @pl.when(z > 0)
-            def _():
-                reduce_line(buf, which, 0, z_dst).wait_recv()
-                add_two(buf, z_dst, from_pair[which, z_dst], from_left[which, z_dst])
-
-            @pl.when(z == 0)
-            def _():
-                add_in(buf, z_dst, from_pair[which, z_dst])
-
-            reduce_line(buf, which, 0, z_dst).start()
-
-        @pl.when(z > z_dst)
-        def _():
-            @pl.when(z < outer - 1)
-            def _():
-                reduce_line(buf, which, 1, z_dst).wait_recv()
-                add_two(buf, z_dst, from_pair[which, z_dst], from_right[which, z_dst])
-
-            @pl.when(z == outer - 1)
-            def _():
-                add_in(buf, z_dst, from_pair[which, z_dst])
-
-            reduce_line(buf, which, 1, z_dst).start()
-
-    def reduce_finish(buf, which, total):
-        total[...] = buf[block(z, y), :].astype(jnp.float32) + from_pair[which, z].astype(
-            jnp.float32
-        )
+        for stream in streams:
+            pair_term = ()
+            if stream == 2:
+                reduce_pair(buf, which, z_dst).wait_recv()
+                pair_term = (from_pair.at[which, z_dst, :, near(which, 1)],)
+            target = home(buf, which, z_dst, stream)
+            for way, ahead, behind in (
+                (0, z < z_dst, z > 0),
+                (1, z > z_dst, z < outer - 1),
+            ):
+
+                @pl.when(ahead & behind)
+                def _(way=way, stream=stream, target=target, pair_term=pair_term):
+                    reduce_line(buf, which, way, z_dst, stream).wait_recv()
+                    add_to(target, landing(which, way, z_dst, stream), *pair_term)
+
+                if stream == 2:
+
+                    @pl.when(ahead & jnp.logical_not(behind))
+                    def _(target=target, pair_term=pair_term):
+                        add_to(target, *pair_term)
+
+                @pl.when(ahead)
+                def _(way=way, stream=stream):
+                    reduce_line(buf, which, way, z_dst, stream).start()
+
+    def reduce_turn(buf, which):
+        target = home(buf, which, z, 1)
 
         @pl.when(z > 0)
         def _():
-            reduce_line(buf, which, 0, z).wait_recv()
-            total[...] += from_left[which, z].astype(jnp.float32)
+            reduce_line(buf, which, 0, z, 1).wait_recv()
+            add_to(target, landing(which, 0, z, 1))
 
         @pl.when(z < outer - 1)
         def _():
-            reduce_line(buf, which, 1, z).wait_recv()
-            total[...] += from_right[which, z].astype(jnp.float32)
+            reduce_line(buf, which, 1, z, 1).wait_recv()
+            add_to(target, landing(which, 1, z, 1))
+
+        reduce_swap(buf, which).start()
+
+    def reduce_finish(buf, which):
+        for stream in (2, 0):
+            cols = near(which, 1) if stream == 2 else far(which, 1)
+            total[:, cols] = home(buf, which, z, stream)[...].astype(jnp.float32)
+
+            @pl.when(z > 0)
+            def _(stream=stream, cols=cols):
+                reduce_line(buf, which, 0, z, stream).wait_recv()
+                total[:, cols] += landing(which, 0, z, stream)[...].astype(jnp.float32)
+
+            @pl.when(z < outer - 1)
+            def _(stream=stream, cols=cols):
+                reduce_line(buf, which, 1, z, stream).wait_recv()
+                total[:, cols] += landing(which, 1, z, stream)[...].astype(jnp.float32)
+
+        reduce_swap(buf, which).wait_recv()
+        total[...] += from_pair[which, z].astype(jnp.float32)
 
     def reduce_drain(buf, which):
         for z_dst in range(outer):
             reduce_pair(buf, which, z_dst).wait_send()
-
-            @pl.when(z < z_dst)
-            def _():
-                reduce_line(buf, which, 0, z_dst).wait_send()
-
-            @pl.when(z > z_dst)
-            def _():
-                reduce_line(buf, which, 1, z_dst).wait_send()
+            for stream in range(3):
+
+                @pl.when(z < z_dst)
+                def _(stream=stream, z_dst=z_dst):
+                    reduce_line(buf, which, 0, z_dst, stream).wait_send()
+
+                @pl.when(z > z_dst)
+                def _(stream=stream, z_dst=z_dst):
+                    reduce_line(buf, which, 1, z_dst, stream).wait_send()
+
+        reduce_swap(buf, which).wait_send()
 
     def columns(index):
         return pl.ds(pl.multiple_of(index * share_cols, share_cols), share_cols)
@@ -481,27 +543,60 @@
             (lax.rem(rep + j, replicas), me),
         )
 
+    tiles = width // COLS
+
+    def tile(index):
+        return pl.ds(pl.multiple_of(index * COLS, COLS), COLS)
+
+    count = x_ref.shape[0]
+    matched = routes_ref[...] == 0
+    flags = jnp.sum(matched.astype(jnp.float32), axis=1, keepdims=True)
+    shares = jnp.sum(
+        jnp.where(matched, weights_ref[...], jnp.float32(0.0)), axis=1, keepdims=True
+    )
+    flag_row = jnp.broadcast_to(flags, (count, count)).T
+    share_row = jnp.broadcast_to(shares, (count, count)).T[:CAP]
+    before = lax.broadcasted_iota(jnp.int32, (count, count), 0)
+    after = lax.broadcasted_iota(jnp.int32, (count, count), 1)
+    upper = (before < after).astype(jnp.bfloat16)
+    flag_row = flag_row[:CAP]
+    places = jnp.dot(flag_row.astype(jnp.bfloat16), upper, preferred_element_type=jnp.float32)
+    slots = lax.broadcasted_iota(jnp.int32, (CAP, count), 0).astype(jnp.float32)
+    chosen = (flag_row > 0.5) & (places == slots)
+    layout = chosen.astype(jnp.float32).astype(jnp.bfloat16)
+    slot_share = jnp.sum(jnp.where(chosen, share_row, 0.0), axis=1, keepdims=True)
+
     mine = block(z, y)
-    xs[mine, :] = x_ref[...]
-    gather_step(xs, 0, 0)
+
+    @pl.loop(0, tiles)
+    def _(t):
+        xs[mine, tile(t)] = jnp.dot(
+            layout, x_ref[:, tile(t)], preferred_element_type=jnp.float32
+        ).astype(jnp.bfloat16)
+
+    pl.semaphore_wait(barrier, groups - 1 + replicas - 1)
+    gather_start(xs, 0)
     frag_order = [replicas // 2] + [j for j in range(1, replicas) if j != replicas // 2]
     for j in frag_order:
         frag_copy(j).start()
     own_piece = pltpu.make_async_copy(fl_ref.at[:, :, columns(rep)], pieces.at[0], frag_own_sem)
     own_piece.start()
-    ys[mine, :] = dy_ref[...]
+    loads[5].wait()
+
+    @pl.loop(0, tiles)
+    def _(t):
+        picked = jnp.dot(layout, grads[:, tile(t)], preferred_element_type=jnp.float32)
+        ys[mine, tile(t)] = (picked * slot_share).astype(jnp.bfloat16)
+
+    gather_turn(xs, 0)
     for hop in range(1, outer - 1):
         gather_step(xs, 0, hop)
-    gather_step(ys, 1, 0)
+    gather_start(ys, 1)
     gather_step(xs, 0, outer - 1)
     loads[0].wait()
     loads[1].wait()
     gather_finish(xs, 0)
-
-    tiles = width // COLS
-
-    def tile(index):
-        return pl.ds(pl.multiple_of(index * COLS, COLS), COLS)
+    gather_turn(ys, 1)
 
     pre[...] = jnp.zeros_like(pre)
 
@@ -516,14 +611,23 @@
     act_t[...] = act.astype(jnp.float32).T.astype(jnp.bfloat16)
     loads[2].wait()
 
-    @pl.loop(0, tiles)
-    def _(t):
+    gather_step(ys, 1, 1)
+    cut = splits[1][0] // COLS
+
+    def forward(t):
         part[:, tile(t)] = jnp.dot(
             hid[...], wd[:, tile(t)], preferred_element_type=jnp.float32
         ).astype(jnp.bfloat16)
 
+    pl.loop(0, cut)(forward)
     reduce_start(part, 0)
-    gather_step(ys, 1, 1)
+    pl.loop(cut, tiles)(forward)
+    reduce_step(part, 0, 0, (1, 0))
+    gather_step(ys, 1, 2)
+    reduce_step(part, 0, 0, (2,))
+    reduce_step(part, 0, 1)
+    for hop in range(3, outer):
+        gather_step(ys, 1, hop)
 
     loads[3].wait()
     own_piece.wait()
@@ -542,10 +646,10 @@
             pseudo[f, rows, :] = value
             return total + jnp.sum(value * value, axis=0, keepdims=True)
 
-        total = lax.fori_loop(
+        squared = lax.fori_loop(
             0, frag_rows // chunk, accumulate, jnp.zeros((1, share_cols), jnp.float32)
         )
-        lanes.append(jnp.sum(total, axis=1, keepdims=True))
+        lanes.append(jnp.sum(squared, axis=1, keepdims=True))
     row_ids = lax.broadcasted_iota(jnp.int32, (8, 128), 0)
     tile_sum = jnp.zeros((8, 128), jnp.float32)
     for f in range(frags):
@@ -554,11 +658,10 @@
     for j in range(1, groups):
         sqe_copy(j).start()
 
-    reduce_step(part, 0, 0)
-    gather_step(ys, 1, 2)
-    reduce_step(part, 0, 1)
-    for hop in range(3, outer):
-        gather_step(ys, 1, hop)
+    for k in range(2, outer):
+        reduce_step(part, 0, k)
+    reduce_turn(part, 0)
+    gather_finish(ys, 1)
 
     for j in range(1, groups):
         sqe_copy(j).wait_recv()
@@ -568,9 +671,6 @@
     sq_part[1] = over_experts
     for j in range(1, replicas):
         sqr_copy(j).start()
-    for k in range(2, outer):
-        reduce_step(part, 0, k)
-    gather_finish(ys, 1)
 
     pre_dact = ggu.at[0]
     pre_dact[...] = jnp.zeros_like(pre_dact)
@@ -586,13 +686,17 @@
     dpre[:, :hidden] = (grad_hidden * pre[:, hidden:] * silu_slope).astype(jnp.bfloat16)
     dpre[:, hidden:] = (grad_hidden * silu_val).astype(jnp.bfloat16)
 
-    @pl.loop(0, tiles)
-    def _(t):
+    cut_dx = splits[1][1] // COLS
+
+    def backward(t):
         part_dx[:, tile(t)] = lax.dot_general(
             dpre[...], wgu[tile(t), :], NT, preferred_element_type=jnp.float32
         ).astype(jnp.bfloat16)
 
+    pl.loop(0, cut_dx)(backward)
     reduce_start(part_dx, 1)
+    pl.loop(cut_dx, tiles)(backward)
+    reduce_step(part_dx, 1, 0, (1, 0))
 
     loads[4].wait()
     for j in range(1, replicas):
@@ -627,10 +731,25 @@
     for store in stores:
         store.start()
 
-    reduce_finish(part, 0, rows_ref)
-    rows_ref[...] = rows_ref[...] * share_ref[...]
-    reduce_step(part_dx, 1, 0)
+    def place(which, ref):
+        total_b = total[...].astype(jnp.bfloat16)
+        for t in range(tiles):
+            cols = pl.ds(t * COLS, COLS)
+            placed[which, :, cols] = lax.dot_general(
+                layout,
+                total_b[:, t * COLS : (t + 1) * COLS],
+                TN,
+                preferred_element_type=jnp.float32,
+            ).astype(jnp.bfloat16)
+        copy = pltpu.make_async_copy(placed.at[which], ref, store_sem.at[5 + which])
+        copy.start()
+        return copy
+
+    reduce_step(part_dx, 1, 0, (2,))
     reduce_step(part_dx, 1, 1)
+    reduce_finish(part, 0)
+    total[...] = total[...] * slot_share
+    placed_out = place(0, lo_ref)
 
     @pl.loop(0, tiles)
     def _(t):
@@ -648,6 +767,7 @@
         store.start()
     for k in range(2, outer):
         reduce_step(part_dx, 1, k)
+    reduce_turn(part_dx, 1)
     gd_out = wd
 
     @pl.loop(0, tiles)
@@ -659,7 +779,8 @@
     last = pltpu.make_async_copy(gd_out, gd_ref, store_sem.at[4])
     last.start()
 
-    reduce_finish(part_dx, 1, dx_ref)
+    reduce_finish(part_dx, 1)
+    placed_dx = place(1, gt_ref)
 
     for buf, which in ((xs, 0), (ys, 1)):
         gather_drain(buf, which)
@@ -673,7 +794,7 @@
         new_copy(j).wait_send()
         new_arrival(j).wait_recv()
     own_new.wait()
-    for store in stores + more + [last]:
+    for store in stores + more + [last, placed_out, placed_dx]:
         store.wait()
 
 
@@ -686,30 +807,17 @@
     width = inputs.shape[1]
     hidden = w_down.shape[1]
     frags, frag_rows, cols = frag_global.shape
-    matched = routes[0] == 0
-    routed = jnp.any(matched, axis=1)
-    share = jnp.sum(jnp.where(matched, cweights[0], jnp.float32(0.0)), axis=1)
-    ahead = jnp.arange(routed.shape[0], dtype=jnp.int32)
-    earlier = (ahead[None, :] <= ahead[:, None]) & routed[None, :]
-    places = jnp.sum(earlier.astype(jnp.int32), axis=1) - 1
-    slot_ids = jnp.arange(CAP, dtype=jnp.int32)
-    layout = routed[None, :] & (places[None, :] == slot_ids[:, None])
-    layout_b = layout.astype(jnp.bfloat16)
-    slot_share = jnp.sum(jnp.where(layout, share[None, :], 0.0), axis=1, keepdims=True)
-    picked = jnp.dot(layout_b, inputs, preferred_element_type=jnp.float32).astype(jnp.bfloat16)
-    dy = jnp.dot(layout_b, grads_in, preferred_element_type=jnp.float32)
-    dy = (dy * slot_share).astype(jnp.bfloat16)
     bf, f32 = jnp.bfloat16, jnp.float32
     outer = groups // INNER
     total = groups * CAP
     dma = pltpu.SemaphoreType.DMA
     vmem, hbm = pl.BlockSpec(memory_space=pltpu.VMEM), pl.BlockSpec(memory_space=pl.ANY)
     shape = jax.ShapeDtypeStruct
-    rows, dx, gg, gu, gd, ng, nm, nl = pl.pallas_call(
-        functools.partial(step_kernel, groups, replicas),
+    lo, gt, gg, gu, gd, ng, nm, nl = pl.pallas_call(
+        functools.partial(step_kernel, groups, replicas, SPLITS),
         out_shape=(
-            shape((CAP, width), f32),
-            shape((CAP, width), f32),
+            shape(inputs.shape, bf),
+            shape(inputs.shape, bf),
             shape((width, hidden), bf),
             shape((width, hidden), bf),
             shape((hidden, width), bf),
@@ -717,16 +825,16 @@
             shape(frag_global.shape, f32),
             shape(frag_local.shape[1:], bf),
         ),
-        in_specs=[vmem] * 3 + [hbm] * 6,
-        out_specs=(vmem,) * 2 + (hbm,) * 6,
+        in_specs=[vmem] * 3 + [hbm] * 7,
+        out_specs=(hbm,) * 8,
         scratch_shapes=[
             pltpu.VMEM((total, width), bf),
             pltpu.VMEM((total, width), bf),
             pltpu.VMEM((total, width), bf),
             pltpu.VMEM((total, width), bf),
             pltpu.VMEM((2, outer, CAP, width), bf),
-            pltpu.VMEM((2, outer, CAP, width), bf),
-            pltpu.VMEM((2, outer, CAP, width), bf),
+            pltpu.VMEM((2, 2, outer, CAP, width), bf),
+            pltpu.VMEM((2, 2, outer, CAP, width), bf),
             pltpu.VMEM((width, 2 * hidden), bf),
             pltpu.VMEM((hidden, width), bf),
             pltpu.VMEM((total, 2 * hidden), f32),
@@ -743,16 +851,19 @@
             pltpu.VMEM((2, 8, 128), f32),
             pltpu.VMEM((groups, 8, 128), f32),
             pltpu.VMEM((replicas, 8, 128), f32),
-            dma((5,)),
-            dma((5,)),
-            dma((2, 2, outer)),
-            dma((2, 2, outer)),
-            dma((2, outer)),
-            dma((2, outer)),
-            dma((2, 2, outer)),
-            dma((2, 2, outer)),
-            dma((2, outer)),
-            dma((2, outer)),
+            pltpu.VMEM((CAP, width), f32),
+            pltpu.VMEM((2, *inputs.shape), bf),
+            pltpu.VMEM(inputs.shape, bf),
+            dma((6,)),
+            dma((7,)),
+            dma((2, 2, 3, outer)),
+            dma((2, 2, 3, outer)),
+            dma((2, outer + 1)),
+            dma((2, outer + 1)),
+            dma((2, 2, 3, outer)),
+            dma((2, 2, 3, outer)),
+            dma((2, outer + 1)),
+            dma((2, outer + 1)),
             dma((replicas,)),
             dma((replicas,)),
             dma,
@@ -768,9 +879,10 @@
             collective_id=0, has_side_effects=True, vmem_limit_bytes=56 * 2**20
         ),
     )(
-        picked,
-        dy,
-        slot_share,
+        inputs,
+        routes[0],
+        cweights[0],
+        grads_in,
         w_gate[0],
         w_up[0],
         w_down[0],
@@ -778,10 +890,7 @@
         frag_global,
         frag_moment,
     )
-    back = layout_b.T
-    layer_out = jnp.dot(back, rows.astype(bf), preferred_element_type=f32).astype(bf)
-    grad_tokens = jnp.dot(back, dx.astype(bf), preferred_element_type=f32).astype(bf)
-    return (layer_out[None], grad_tokens[None], gg[None], gu[None], gd[None], ng, nm, nl[None])
+    return (lo[None], gt[None], gg[None], gu[None], gd[None], ng, nm, nl[None])
 
 
 def body(*operands):

time: 137 us -> 122 us (0.89); the launches traced: 136 us -> 122 us
  Pallas kernels: 118 us -> 109 us
  matrix products: 8.34 us -> 0 us
  local copies, waits for them, and re-layouts: 7.22 us -> 12.6 us
    pallas_call x1, Pallas kernels: 118 us -> 109 us  [pair_body(): pl.pallas_call(functools.partial(step_kernel, groups, replicas, SPLITS),...]
    dot_general x4 -> x0, matrix products: 8.34 us -> none  [the longest x1 2.58 us: pair_body(): jnp.dot(back, dx.astype(bf), preferred_element_type=f32).astype(bf)]
    unnamed x20 -> x24, local copies, waits for them, and re-layouts: 6.53 us -> 12.6 us
where the time goes in v2:
time: 122 us
  Pallas kernels  109 us (89%)
  local copies, waits for them, and re-layouts  12.6 us (10%)
    pallas_call x1, Pallas kernels, pair_body(): pl.pallas_call(functools.partial(step_kernel, groups, replicas, SPLITS),...  109 us
    unnamed x24, local copies, waits for them, and re-layouts  12.6 us

profile of v2, /device:TPU:16, one launch (start us, length us, event | category | flops | bytes accessed | tf_op | source)
XLA Modules:
  0.0 122.1 jit_solution(14916336029422262863)
XLA Ops:
  0.6 1.4 %copy.18 = s32[1,128,8]{2,1,0:T(8,128)} copy(s32[1,128,8]{1,2,0:T(8,128)} %param.11) | data formatting | bytes 8192 | tf_op args[1]
  2.0 1.4 %copy.19 = f32[1,128,8]{2,1,0:T(8,128)} copy(f32[1,128,8]{1,2,0:T(8,128)} %param.12) | data formatting | bytes 8192 | tf_op args[2]
  3.5 108.8 %shard_map.161 = (bf16[128,4096]{1,0:T(8,128)(2,1)}, bf16[128,4096]{1,0:T(8,128)(2,1)}, bf16[4096,128]{1,0:T(8,128)(2,1)}, bf16[4096,128]{1,0:T(8,128)(2,1)}, bf...) custom-call(bf16[128,4096]{1,0:T(8,128)(2,1)} %bitcast.16, ...), custom_call_target="tpu_custom_call" | custom-call | tf_op jit(solution)/shard_map/pallas_call | solution.py:816
  112.3 0.0 copy-start.6
  112.3 0.0 copy-start.5
  112.3 2.4 %copy.28 = bf16[1,128,4096]{2,1,0:T(8,128)(2,1)} copy(bf16[1,128,4096]{2,1,0:T(8,128)(2,1)} %bitcast.25) | data formatting | bytes 2097152
  114.7 0.0 copy-done.6
  114.7 0.0 copy-start.4
  114.8 1.0 copy.29
  115.7 0.0 copy-done.5
  115.7 0.0 copy-start.3
  115.7 1.0 copy.30
  116.7 0.0 copy-done.4
  116.7 0.0 copy-start.2
  116.7 1.0 copy.31
  117.7 0.0 copy-done.3
  117.7 0.0 copy-start.1
  117.7 1.0 copy.32
  118.6 0.0 copy-done.2
  118.7 1.0 copy.33
  119.6 0.0 copy-done.1
  119.6 1.0 copy.34
  120.6 0.1 copy-done
  120.7 1.3 %copy.35 = bf16[1,2,128,4096]{3,2,1,0:T(8,128)(2,1)} copy(bf16[1,2,128,4096]{3,2,1,0:T(8,128)(2,1)S(1)} %bitcast.14) | data formatting | bytes 4194304
  (1 shorter events, 0.0 us)
Async XLA Ops:
  112.3 2.5 %copy-start.6 = (bf16[128,4096]{1,0:T(8,128)(2,1)S(1)}, bf16[128,4096]{1,0:T(8,128)(2,1)}, u32[]{:S(2)}) copy-start(bf16[128,4096]{1,0:T(8,128)(2,1)} %get-tuple-element.17) | copy-start | bytes 3145732
  112.3 3.4 %copy-start.5 = (bf16[4096,128]{1,0:T(8,128)(2,1)S(1)}, bf16[4096,128]{1,0:T(8,128)(2,1)}, u32[]{:S(2)}) copy-start(bf16[4096,128]{1,0:T(8,128)(2,1)} %get-tuple-element.18) | copy-start | bytes 3145732
  114.7 1.9 %copy-start.4 = (bf16[4096,128]{1,0:T(8,128)(2,1)S(1)}, bf16[4096,128]{1,0:T(8,128)(2,1)}, u32[]{:S(2)}) copy-start(bf16[4096,128]{1,0:T(8,128)(2,1)} %get-tuple-element.19) | copy-start | bytes 3145732
  115.7 1.9 %copy-start.3 = (bf16[128,4096]{1,0:T(8,128)(2,1)S(1)}, bf16[128,4096]{1,0:T(8,128)(2,1)}, u32[]{:S(2)}) copy-start(bf16[128,4096]{1,0:T(8,128)(2,1)} %get-tuple-element.20) | copy-start | bytes 3145732
  116.7 1.9 %copy-start.2 = (f32[2,128,1024]{2,1,0:T(8,128)S(1)}, f32[2,128,1024]{2,1,0:T(8,128)}, u32[]{:S(2)}) copy-start(f32[2,128,1024]{2,1,0:T(8,128)} %get-tuple-element.37) | copy-start | bytes 3145732
  117.7 1.9 %copy-start.1 = (f32[2,128,1024]{2,1,0:T(8,128)S(1)}, f32[2,128,1024]{2,1,0:T(8,128)}, u32[]{:S(2)}) copy-start(f32[2,128,1024]{2,1,0:T(8,128)} %get-tuple-element.38) | copy-start | bytes 3145732
  118.6 2.1 %copy-start = (bf16[2,128,4096]{2,1,0:T(8,128)(2,1)S(1)}, bf16[2,128,4096]{2,1,0:T(8,128)(2,1)}, u32[]{:S(2)}) copy-start(bf16[2,128,4096]{2,1,0:T(8,128)(2,1)} %get-tuple-element.23) | copy-start | bytes 6291460

commit v3 on v2

--- a/solution.py
+++ b/solution.py
@@ -550,16 +550,15 @@
 
     count = x_ref.shape[0]
     matched = routes_ref[...] == 0
-    flags = jnp.sum(matched.astype(jnp.float32), axis=1, keepdims=True)
-    shares = jnp.sum(
-        jnp.where(matched, weights_ref[...], jnp.float32(0.0)), axis=1, keepdims=True
+    flag_row = jnp.broadcast_to(
+        jnp.sum(matched.astype(jnp.float32), axis=0, keepdims=True), (CAP, count)
     )
-    flag_row = jnp.broadcast_to(flags, (count, count)).T
-    share_row = jnp.broadcast_to(shares, (count, count)).T[:CAP]
+    share_row = jnp.sum(
+        jnp.where(matched, weights_ref[...], jnp.float32(0.0)), axis=0, keepdims=True
+    )
     before = lax.broadcasted_iota(jnp.int32, (count, count), 0)
     after = lax.broadcasted_iota(jnp.int32, (count, count), 1)
     upper = (before < after).astype(jnp.bfloat16)
-    flag_row = flag_row[:CAP]
     places = jnp.dot(flag_row.astype(jnp.bfloat16), upper, preferred_element_type=jnp.float32)
     slots = lax.broadcasted_iota(jnp.int32, (CAP, count), 0).astype(jnp.float32)
     chosen = (flag_row > 0.5) & (places == slots)
@@ -880,8 +879,8 @@
         ),
     )(
         inputs,
-        routes[0],
-        cweights[0],
+        routes[0].T,
+        cweights[0].T,
         grads_in,
         w_gate[0],
         w_up[0],

time: 122 us -> 119 us (0.975)
  local copies, waits for them, and re-layouts: 12.6 us -> 9.75 us
    unnamed x24 -> x22, local copies, waits for them, and re-layouts: 12.6 us -> 9.75 us
where the time goes in v3:
time: 119 us
  Pallas kernels  108 us (91%)
  local copies, waits for them, and re-layouts  9.75 us (8%)
    pallas_call x1, Pallas kernels, pair_body(): pl.pallas_call(functools.partial(step_kernel, groups, replicas, SPLITS),...  108 us
    unnamed x22, local copies, waits for them, and re-layouts  9.75 us

profile of v3, /device:TPU:16, one launch (start us, length us, event | category | flops | bytes accessed | tf_op | source)
XLA Modules:
  0.0 118.8 jit_solution(9922073546765815025)
XLA Ops:
  0.6 108.4 %shard_map.161 = (bf16[128,4096]{1,0:T(8,128)(2,1)}, bf16[128,4096]{1,0:T(8,128)(2,1)}, bf16[4096,128]{1,0:T(8,128)(2,1)}, bf16[4096,128]{1,0:T(8,128)(2,1)}, bf...) custom-call(bf16[128,4096]{1,0:T(8,128)(2,1)} %bitcast.25, ...), custom_call_target="tpu_custom_call" | custom-call | tf_op jit(solution)/shard_map/pallas_call | solution.py:815
  109.0 0.0 copy-start.6
  109.1 0.0 copy-start.5
  109.1 2.4 %copy.26 = bf16[1,128,4096]{2,1,0:T(8,128)(2,1)} copy(bf16[1,128,4096]{2,1,0:T(8,128)(2,1)} %bitcast.24) | data formatting | bytes 2097152
  111.5 0.0 copy-done.6
  111.5 0.0 copy-start.4
  111.5 1.0 copy.27
  112.5 0.0 copy-done.5
  112.5 0.0 copy-start.3
  112.5 1.0 copy.28
  113.4 0.0 copy-done.4
  113.4 0.0 copy-start.2
  113.5 1.0 copy.29
  114.4 0.0 copy-done.3
  114.4 0.0 copy-start.1
  114.4 1.0 copy.30
  115.4 0.0 copy-done.2
  115.4 0.0 copy-start
  115.4 1.0 copy.31
  116.4 0.0 copy-done.1
  116.4 1.0 copy.32
  117.3 0.1 copy-done
  117.5 1.3 %copy.33 = bf16[1,2,128,4096]{3,2,1,0:T(8,128)(2,1)} copy(bf16[1,2,128,4096]{3,2,1,0:T(8,128)(2,1)S(1)} %bitcast.18) | data formatting | bytes 4194304
Async XLA Ops:
  109.0 2.5 %copy-start.6 = (bf16[128,4096]{1,0:T(8,128)(2,1)S(1)}, bf16[128,4096]{1,0:T(8,128)(2,1)}, u32[]{:S(2)}) copy-start(bf16[128,4096]{1,0:T(8,128)(2,1)} %get-tuple-element.17) | copy-start | bytes 3145732
  109.1 3.4 %copy-start.5 = (bf16[4096,128]{1,0:T(8,128)(2,1)S(1)}, bf16[4096,128]{1,0:T(8,128)(2,1)}, u32[]{:S(2)}) copy-start(bf16[4096,128]{1,0:T(8,128)(2,1)} %get-tuple-element.18) | copy-start | bytes 3145732
  111.5 1.9 %copy-start.4 = (bf16[4096,128]{1,0:T(8,128)(2,1)S(1)}, bf16[4096,128]{1,0:T(8,128)(2,1)}, u32[]{:S(2)}) copy-start(bf16[4096,128]{1,0:T(8,128)(2,1)} %get-tuple-element.19) | copy-start | bytes 3145732
  112.5 1.9 %copy-start.3 = (bf16[128,4096]{1,0:T(8,128)(2,1)S(1)}, bf16[128,4096]{1,0:T(8,128)(2,1)}, u32[]{:S(2)}) copy-start(bf16[128,4096]{1,0:T(8,128)(2,1)} %get-tuple-element.20) | copy-start | bytes 3145732
  113.4 1.9 %copy-start.2 = (f32[2,128,1024]{2,1,0:T(8,128)S(1)}, f32[2,128,1024]{2,1,0:T(8,128)}, u32[]{:S(2)}) copy-start(f32[2,128,1024]{2,1,0:T(8,128)} %get-tuple-element.37) | copy-start | bytes 3145732
  114.4 1.9 %copy-start.1 = (f32[2,128,1024]{2,1,0:T(8,128)S(1)}, f32[2,128,1024]{2,1,0:T(8,128)}, u32[]{:S(2)}) copy-start(f32[2,128,1024]{2,1,0:T(8,128)} %get-tuple-element.38) | copy-start | bytes 3145732
  115.4 2.1 %copy-start = (bf16[2,128,4096]{2,1,0:T(8,128)(2,1)S(1)}, bf16[2,128,4096]{2,1,0:T(8,128)(2,1)}, u32[]{:S(2)}) copy-start(bf16[2,128,4096]{2,1,0:T(8,128)(2,1)} %get-tuple-element.23) | copy-start | bytes 6291460
